TPU v7x, 32 devices: a whole 2x2x4 slice. The times are simulated.
32 devices in a mesh: grp: 2 (over y), dp: 16 (over z, x, core).
Axes of the slice: x: 2, y: 2, z: 4, core: 2. Of those that a mesh axis runs over, the one named last changes fastest.
Arguments:
- acts: bfloat16 [16384, 2560], P(('grp', 'dp')), may hold values from -18 to 18
- cotangents: bfloat16 [16384, 768], P(('grp', 'dp')), may hold values from -6 to 6
Outputs:
- update: float32 [2560, 768], P(('grp', 'dp'))
All inputs are finite; a program needn't handle non-finite values. Where the computation divides by a largest or mean magnitude, that divisor is 1e-20 or more.
Results may differ from a plain program's by a relative error of at most 0.013.
Values may be sent and summed in bfloat16 or wider, within the bound.
A program may use at most 64 MiB of HBM per device.

v0:
```python
import functools

import jax
import jax.numpy as jnp
from jax import lax
from jax.experimental import pallas as pl
from jax.experimental.pallas import tpu as pltpu
from jax.sharding import PartitionSpec as P

D = 2560
R = 768
BLK = 128
ITERS = 8
NA = D // BLK
NG = R // BLK
QROWS = D // 4
QBLK = QROWS // BLK
HALF = QROWS // 2
CCOLS = R // 2
CBLK = CCOLS // BLK
SLOTS = 4
MESH = pl.DeviceIdType.MESH
F32 = jnp.float32
BF16 = jnp.bfloat16


def dot(a, b):
    return jnp.dot(a, b, preferred_element_type=F32)


def dot_t(a, b):
    return lax.dot_general(a, b, (((0,), (0,)), ((), ())), preferred_element_type=F32)


def split(a):
    hi = a.astype(BF16)
    return hi, (a - hi.astype(F32)).astype(BF16)


def dot3(a, b):
    ah, al = split(a)
    bh, bl = split(b)
    return dot(jnp.concatenate([ah, ah, al], axis=1), jnp.concatenate([bh, bl, bh], axis=0))


def kernel(
    groups, width, total, rows,
    x_hbm, g_hbm, out_ref,
    x_ref, g_ref, xt, fpart, f1recv, f2send, f2recv, f3send, f3recv,
    m1send, m1recv, macc, m2a, m2s, m2b, mq,
    zsend, zrecv, inv_own, inv_a, inv_g, nat, fin_send, fin_recv, qsend, q1recv, q2recv,
    in_sem,
    f1_ss, f1_rs, f2_ss, f2_rs, f3_ss, f3_rs, m1_ss, m1_rs, ma_ss, ma_rs,
    mb_ss, mb_rs, z_ss, z_rs, inv_ss, inv_rs, fin_ss, fin_rs, q1_ss, q1_rs, q2_ss, q2_rs,
):
    devices = groups * width
    rest_n = devices // 8
    owners = devices // 4
    half_n = devices // 2
    zslots = zsend.shape[1]
    pieces = fin_send.shape[0] // zslots
    dp_rest = width // 4
    gi = lax.axis_index("grp")
    di = lax.axis_index("dp")
    me = gi * width + di
    core = lax.rem(di, 2)
    x = lax.rem(lax.div(di, 2), 2)
    y = lax.rem(gi, 2)
    q = 2 * y + x
    rest = lax.div(gi, 2) * dp_rest + lax.div(di, 4)

    def at(yy, xx, zz, cc):
        return (
            lax.div(zz, dp_rest) * 2 + yy,
            lax.rem(zz, dp_rest) * 4 + xx * 2 + cc,
        )

    def linear(d):
        return (lax.div(d, width), lax.rem(d, width))

    def rcopy(src, dst, ss, rs, dev):
        return pltpu.make_async_remote_copy(
            src_ref=src, dst_ref=dst, send_sem=ss, recv_sem=rs,
            device_id=dev, device_id_type=MESH,
        )

    g_in = pltpu.make_async_copy(g_hbm, g_ref, in_sem.at[4])
    g_in.start()
    x_in = []
    for i in range(4):
        cols = pl.ds(i * QROWS, QROWS)
        x_in.append(pltpu.make_async_copy(x_hbm.at[:, cols], x_ref.at[:, cols], in_sem.at[i]))
        x_in[i].start()

    barrier = pltpu.get_barrier_semaphore()

    def greet(dev):
        pl.semaphore_signal(barrier, inc=1, device_id=dev, device_id_type=MESH)

    greet(at(y, x, rest, 1 - core))
    for yy, xx in ((y, 1 - x), (1 - y, x), (1 - y, 1 - x)):
        greet(at(yy, xx, rest, core))

    @pl.loop(0, rest_n)
    def _(z):
        @pl.when(z != rest)
        def _():
            greet(at(y, x, z, core))

    zero = jnp.zeros((BLK, BLK), BF16)
    g_in.wait()
    for c in range(NG):
        gb = g_ref[:, c * BLK:(c + 1) * BLK]
        fg = dot_t(gb, gb).astype(BF16)
        if c < 4:
            fpart[1, c, 2] = fg
        else:
            fpart[0, c - 4, 3] = fg
    for c in range(4):
        fpart[1, c, 3] = zero
        if c >= NG - 4:
            fpart[0, c, 3] = zero

    for part in range(4):
        x_in[part].wait()
        for b in range(part * QBLK, (part + 1) * QBLK):
            qq, t = b // (2 * QBLK) * 2 + b % 2, b % (2 * QBLK) // 2
            xb = x_ref[:, b * BLK:(b + 1) * BLK]
            xbt = xb.T
            xt[qq * QBLK + t] = xbt
            fpart[t % 2, qq, t // 2] = dot(xbt, xb).astype(BF16)

    pl.semaphore_wait(barrier, rest_n + 3)
    other = at(y, x, rest, 1 - core)
    f1 = rcopy(fpart.at[1 - core], f1recv, f1_ss.at[0], f1_rs.at[0], other)
    f1.start()

    g_other = g_ref[:, pl.ds(pl.multiple_of((1 - core) * CCOLS, BLK), CCOLS)]

    def m1_copy(qq):
        return rcopy(m1send.at[qq], m1recv.at[qq], m1_ss.at[qq], m1_rs.at[qq], other)

    @pl.loop(1, 5)
    def _(turn):
        qq = lax.rem(q + turn, 4)
        for t in range(QBLK):
            m1send[qq, t * BLK:(t + 1) * BLK, :] = dot(xt[qq * QBLK + t], g_other).astype(BF16)
        m1_copy(qq).start()

    f1.wait_recv()

    def f1_sum(qq, s):
        return fpart[core, qq, s].astype(F32) + f1recv[qq, s].astype(F32)

    chips = [(y, 1 - x), (1 - y, x), (1 - y, 1 - x)]
    f2 = []
    for k, (yy, xx) in enumerate(chips):
        qq = 2 * yy + xx
        for s in range(SLOTS):
            f2send[k, s] = f1_sum(qq, s).astype(BF16)
        c2 = rcopy(f2send.at[k], f2recv.at[k], f2_ss.at[k], f2_rs.at[k], at(yy, xx, rest, core))
        c2.start()
        f2.append(c2)

    g_mine = g_ref[:, pl.ds(pl.multiple_of(core * CCOLS, BLK), CCOLS)]

    at_x = at(y, 1 - x, rest, core)
    at_y = at(1 - y, x, rest, core)

    def ma_copy(i, h):
        quarter = 2 * i + (1 - x) if h == 0 else 2 * (1 - y) + i
        k = 2 * h + i
        return rcopy(
            macc.at[quarter, pl.ds(h * HALF, HALF)], m2a.at[k],
            ma_ss.at[k], ma_rs.at[k], at_x if h == 0 else at_y,
        )

    @pl.loop(1, 5)
    def _(turn):
        qq = lax.rem(q + turn, 4)
        m1_copy(qq).wait_recv()
        for t in range(QBLK):
            part = dot(xt[qq * QBLK + t], g_mine)
            sl = slice(t * BLK, (t + 1) * BLK)
            macc[qq, sl, :] = (part + m1recv[qq, sl, :].astype(F32)).astype(BF16)
        yq, xq = lax.div(qq, 2), lax.rem(qq, 2)

        @pl.when(xq != x)
        def _():
            ma_copy(yq, 0).start()

        @pl.when(yq != y)
        def _():
            ma_copy(xq, 1).start()

    ma = [ma_copy(i, h) for i in range(2) for h in range(2)]

    for c2 in f2:
        c2.wait_recv()
    for s in range(SLOTS):
        f = f1_sum(q, s)
        for k in range(3):
            f = f + f2recv[k, s].astype(F32)
        f3send[s] = f.astype(BF16)

    def f3_copy(s, src):
        return rcopy(f3send.at[s], f3recv.at[src], f3_ss.at[s], f3_rs.at[src], at(y, x, s, core))

    for s in range(SLOTS):
        @pl.when(rest != s)
        def _():
            f3_copy(s, rest).start()

    f3recv[rest] = f3send[lax.rem(rest, SLOTS)]

    @pl.when(rest < SLOTS)
    def _():
        @pl.loop(0, rest_n)
        def _(z):
            @pl.when(z != rest)
            def _():
                f3_copy(0, z).wait_recv()

    if rest_n > SLOTS:
        @pl.when(rest >= SLOTS)
        def _():
            @pl.loop(0, rest_n)
            def _(z):
                f3recv[z] = zero

    factor = f3recv[0].astype(F32)
    for z in range(1, rest_n):
        factor = factor + f3recv[z].astype(F32)
    factor = factor * (1.0 / total)

    eye = (
        lax.broadcasted_iota(jnp.int32, (BLK, BLK), 0)
        == lax.broadcasted_iota(jnp.int32, (BLK, BLK), 1)
    ).astype(F32)
    trace = jnp.sum(jnp.sum(factor * eye, axis=1, keepdims=True), axis=0, keepdims=True)
    damped = factor + (0.1 * (trace / BLK + 1e-06)) * eye
    peak = jnp.max(jnp.sum(jnp.abs(damped), axis=1, keepdims=True), axis=0, keepdims=True)
    scale = 1.0 / peak
    approx = scale * (2.0 * eye - scale * damped)
    for _ in range(ITERS - 5):
        approx = dot3(approx, 2.0 * eye - dot3(damped, approx))

    for ca in ma:
        ca.wait_recv()
    for i in range(2):
        for h in range(2):
            k = 2 * h + i
            quarter = 2 * i + x if h == 0 else 2 * y + i
            m2s[k] = (
                macc[quarter, h * HALF:(h + 1) * HALF, :].astype(F32) + m2a[k].astype(F32)
            ).astype(BF16)
    mb = [
        rcopy(m2s.at[1 - y], m2b.at[0], mb_ss.at[0], mb_rs.at[0], at_y),
        rcopy(m2s.at[2 + 1 - x], m2b.at[1], mb_ss.at[1], mb_rs.at[1], at_x),
    ]
    for cb in mb:
        cb.start()

    for _ in range(4):
        approx = dot3(approx, 2.0 * eye - dot3(damped, approx))
    inv_own[...] = approx.astype(BF16)

    slot = 2 * rest + core
    is_a = slot < QBLK
    is_g = jnp.logical_or(slot == QBLK, jnp.logical_and(slot == QBLK + 1, q < NG - 4))
    gidx = (slot - QBLK) * 4 + q
    ghalf = lax.div(gidx, CBLK)

    def a_copy(i, t):
        return rcopy(
            inv_own, inv_a.at[t], inv_ss.at[i], inv_rs.at[t],
            at(y, x, lax.div(i, 2), lax.rem(i, 2)),
        )

    def g_dev(i):
        chip = lax.div(i, rest_n)
        return at(lax.div(chip, 2), lax.rem(chip, 2), lax.rem(i, rest_n), ghalf)

    def g_copy(i, c):
        return rcopy(inv_own, inv_g.at[c], inv_ss.at[i], inv_rs.at[QBLK + c], g_dev(i))

    def not_me(i):
        gg, dd = g_dev(i)
        return gg * width + dd != me

    @pl.when(is_a)
    def _():
        @pl.loop(0, owners)
        def _(i):
            @pl.when(i != slot)
            def _():
                a_copy(i, slot).start()
        inv_a[slot] = inv_own[...]

    @pl.when(is_g)
    def _():
        @pl.loop(0, 4 * rest_n)
        def _(i):
            @pl.when(not_me(i))
            def _():
                g_copy(i, lax.rem(gidx, CBLK)).start()

        @pl.when(ghalf == core)
        def _():
            inv_g[lax.rem(gidx, CBLK)] = inv_own[...]

    for cb in mb:
        cb.wait_recv()
    for h in range(2):
        kept = m2s[y] if h == 0 else m2s[2 + x]
        mq[h * HALF:(h + 1) * HALF, :] = (
            (kept.astype(F32) + m2b[h].astype(F32)) * (1.0 / total)
        ).astype(BF16)

    for i in range(zslots * rest_n):
        t, c = divmod(i, CBLK)
        tile = zero if t >= QBLK else mq[t * BLK:(t + 1) * BLK, c * BLK:(c + 1) * BLK]
        zsend[i // zslots, i % zslots] = tile

    def z_copy(dst, src):
        return rcopy(zsend.at[dst], zrecv.at[src], z_ss.at[dst], z_rs.at[src], at(y, x, dst, core))

    @pl.loop(0, rest_n)
    def _(z):
        @pl.when(z != rest)
        def _():
            z_copy(z, rest).start()

    zrecv[rest] = zsend[rest]

    for c in range(CBLK):
        @pl.when(jnp.logical_not(jnp.logical_and(is_g, gidx == core * CBLK + c)))
        def _():
            g_copy(0, c).wait_recv()
    for t in range(QBLK):
        @pl.when(slot != t)
        def _():
            a_copy(0, t).wait_recv()

    @pl.loop(0, rest_n)
    def _(z):
        @pl.when(z != rest)
        def _():
            z_copy(0, z).wait_recv()

    square = jnp.zeros((1, 1), F32)
    for k in range(zslots):
        tile = rest * zslots + k
        m = zrecv[0, k].astype(F32)
        for z in range(1, rest_n):
            m = m + zrecv[z, k].astype(F32)
        left = dot_t(inv_a[jnp.minimum(lax.div(tile, CBLK), QBLK - 1)], m.astype(BF16))
        hi, lo = split(left)
        ginv = inv_g[lax.rem(tile, CBLK)]
        part = dot(hi, ginv) + dot(lo, ginv)
        nat[k] = part
        square = square + jnp.sum(
            jnp.sum(part * part, axis=0, keepdims=True), axis=1, keepdims=True
        )
    qsend[0] = jnp.broadcast_to(square, (8, 128))

    def q1_copy(p, src):
        return rcopy(
            qsend.at[0], q1recv.at[src], q1_ss.at[p], q1_rs.at[src],
            at(lax.div(p, 4), lax.rem(lax.div(p, 2), 2), rest, lax.rem(p, 2)),
        )

    def q2_copy(z, src):
        return rcopy(qsend.at[1], q2recv.at[src], q2_ss.at[z], q2_rs.at[src], at(y, x, z, core))

    plane = 2 * q + core

    def others(n, mine, body):
        @pl.loop(0, n)
        def _(p):
            @pl.when(p != mine)
            def _():
                body(p)

    others(8, plane, lambda p: q1_copy(p, plane).start())
    q1recv[plane] = qsend[0]

    def each_piece(body):
        for xx in range(2):
            for i in range(QBLK * CBLK):
                t, c = divmod(i, CBLK)
                top = (2 * t + xx) * BLK

                @pl.when(jnp.logical_and(x == xx, rest == i // zslots))
                def _():
                    first = top // rows
                    for k in range(first, (top + BLK + rows - 1) // rows):
                        lo, hi = max(top, k * rows), min(top + BLK, (k + 1) * rows)
                        late = 0 if lo == k * rows else 1
                        body(i % zslots, c, k, lo - k * rows, lo - top, hi - lo, late,
                             i % zslots * pieces + k - first)

    def fin_copy(j, c, late, k):
        return rcopy(
            fin_send.at[j], fin_recv.at[core * CBLK + c, late], fin_ss.at[j],
            fin_rs.at[2 * (core * CBLK + c) + late], linear(y * half_n + k),
        )

    def send_piece(slot_k, c, k, above, start, count, late, j):
        parts = [nat[slot_k, start:start + count, :]]
        if above:
            parts.insert(0, jnp.zeros((above, BLK), F32))
        tail = fin_send.shape[1] - above - count
        if tail:
            parts.append(jnp.zeros((tail, BLK), F32))
        fin_send[j] = (jnp.concatenate(parts, axis=0) if len(parts) > 1 else parts[0]).astype(BF16)

        @pl.when(y * half_n + k != me)
        def _():
            fin_copy(j, c, late, k).start()

        @pl.when(y * half_n + k == me)
        def _():
            fin_recv[core * CBLK + c, late] = fin_send[j]

    each_piece(send_piece)

    others(8, plane, lambda p: q1_copy(0, p).wait_recv())
    qsend[1] = jnp.sum(q1recv[...], axis=0)
    others(rest_n, rest, lambda z: q2_copy(z, rest).start())
    q2recv[rest] = qsend[1]

    k_me = lax.rem(me, half_n)
    t_me = lax.div(k_me * rows, BLK)
    straddles = lax.div(k_me * rows + rows - 1, BLK) > t_me
    mine_here = lax.div(me, half_n) == y
    for late in range(2):
        for c in range(NG):
            from_me = jnp.logical_and(
                jnp.logical_and(mine_here, core == c // CBLK),
                jnp.logical_and(
                    lax.rem(t_me + late, 2) == x,
                    lax.div(CBLK * lax.div(t_me + late, 2) + c % CBLK, zslots) == rest,
                ),
            )
            incoming = jnp.logical_not(from_me)
            if late:
                incoming = jnp.logical_and(straddles, incoming)

                @pl.when(jnp.logical_not(straddles))
                def _():
                    fin_recv[c, 1] = jnp.zeros(fin_recv.shape[2:], BF16)

            @pl.when(incoming)
            def _():
                pltpu.make_async_remote_copy(
                    src_ref=fin_send.at[0], dst_ref=fin_recv.at[c, late], send_sem=fin_ss.at[0],
                    recv_sem=fin_rs.at[2 * c + late], device_id=other, device_id_type=MESH,
                ).wait_recv()

    others(rest_n, rest, lambda z: q2_copy(0, z).wait_recv())
    quad = jnp.sum(q2recv[...], axis=0)[:1, :1] / (D * R)
    factor_out = lax.rsqrt(quad + 1e-06)
    for c in range(NG):
        natural = fin_recv[c, 0].astype(F32) + fin_recv[c, 1].astype(F32)
        out_ref[:, c * BLK:(c + 1) * BLK] = natural[:rows, :] * factor_out

    f1.wait_send()
    for cp in f2 + ma + mb:
        cp.wait_send()

    @pl.loop(0, 4)
    def _(qq):
        m1_copy(qq).wait_send()

    for s in range(SLOTS):
        @pl.when(rest != s)
        def _():
            f3_copy(s, rest).wait_send()

    @pl.when(is_a)
    def _():
        @pl.loop(0, owners)
        def _(i):
            @pl.when(i != slot)
            def _():
                a_copy(i, 0).wait_send()

    @pl.when(is_g)
    def _():
        @pl.loop(0, 4 * rest_n)
        def _(i):
            @pl.when(not_me(i))
            def _():
                g_copy(i, 0).wait_send()

    others(rest_n, rest, lambda z: z_copy(z, 0).wait_send())
    others(8, plane, lambda p: q1_copy(p, 0).wait_send())
    others(rest_n, rest, lambda z: q2_copy(z, 0).wait_send())

    def wait_piece(slot_k, c, k, above, start, count, late, j):
        @pl.when(y * half_n + k != me)
        def _():
            fin_copy(j, c, late, k).wait_send()

    each_piece(wait_piece)


def per_device(acts, cotangents, groups, width):
    tokens = acts.shape[0]
    devices = groups * width
    rest_n = devices // 8
    owners = devices // 4
    rows = D // devices
    padded = (rows + 15) // 16 * 16
    blk = (BLK, BLK)
    zslots = (QBLK * CBLK + rest_n - 1) // rest_n
    pieces = max(
        ((t + 1) * BLK + rows - 1) // rows - t * BLK // rows for t in range(2 * QBLK)
    )
    sems = [5, 1, 1, 3, 3, SLOTS, rest_n, 4, 4, 4, 4, 2, 2, rest_n, rest_n, max(owners, 4 * rest_n),
            QBLK + CBLK, zslots * pieces, 2 * NG, 8, 8, rest_n, rest_n]
    vm = pltpu.VMEM
    return pl.pallas_call(
        functools.partial(kernel, groups, width, tokens * devices, rows),
        out_shape=jax.ShapeDtypeStruct((rows, R), F32),
        in_specs=[pl.BlockSpec(memory_space=pl.ANY)] * 2,
        out_specs=pl.BlockSpec(memory_space=pltpu.VMEM),
        scratch_shapes=[
            vm((tokens, D), BF16),
            vm((tokens, R), BF16),
            vm((NA, BLK, tokens), BF16),
            vm((2, 4, SLOTS) + blk, BF16),
            vm((4, SLOTS) + blk, BF16),
            vm((3, SLOTS) + blk, BF16),
            vm((3, SLOTS) + blk, BF16),
            vm((SLOTS,) + blk, BF16),
            vm((rest_n,) + blk, BF16),
            vm((4, QROWS, CCOLS), BF16),
            vm((4, QROWS, CCOLS), BF16),
            vm((4, QROWS, CCOLS), BF16),
            vm((4, HALF, CCOLS), BF16),
            vm((4, HALF, CCOLS), BF16),
            vm((2, HALF, CCOLS), BF16),
            vm((QROWS, CCOLS), BF16),
            vm((rest_n, zslots) + blk, BF16),
            vm((rest_n, zslots) + blk, BF16),
            vm(blk, BF16),
            vm((QBLK,) + blk, BF16),
            vm((CBLK,) + blk, BF16),
            vm((zslots,) + blk, F32),
            vm((zslots * pieces, padded, BLK), BF16),
            vm((NG, 2, padded, BLK), BF16),
            vm((2, 8, 128), F32),
            vm((8, 8, 128), F32),
            vm((rest_n, 8, 128), F32),
        ] + [pltpu.SemaphoreType.DMA((n,)) for n in sems],
        compiler_params=pltpu.CompilerParams(
            collective_id=0, has_side_effects=True, vmem_limit_bytes=48 * 1024 * 1024
        ),
    )(acts, cotangents)


def solution(mesh):
    groups, width = mesh.shape["grp"], mesh.shape["dp"]
    spec = P(("grp", "dp"), None)
    return jax.shard_map(
        functools.partial(per_device, groups=groups, width=width),
        mesh=mesh, in_specs=(spec, spec), out_specs=spec, check_vma=False,
    )
```

profile of v0, /device:TPU:0, one launch (start us, length us, event | category | flops | bytes accessed | tf_op | source)
XLA Modules:
  0.0 60.2 jit_solution(6720828504485472905)
XLA Ops:
  0.0 0.0 copy-start
  0.0 1.7 %copy-done = bf16[512,2560]{1,0:T(8,128)(2,1)S(1)} copy-done((bf16[512,2560]{1,0:T(8,128)(2,1)S(1)}, bf16[512,2560]{1,0:T(8,128)(2,1)}, u32[]{:S(2)}) %copy-start) | copy-done | bytes 2621464
  1.7 0.0 copy-start.1
  1.7 1.1 %copy-done.1 = bf16[512,768]{1,0:T(8,128)(2,1)S(1)} copy-done((bf16[512,768]{1,0:T(8,128)(2,1)S(1)}, bf16[512,768]{1,0:T(8,128)(2,1)}, u32[]{:S(2)}) %copy-start.1) | copy-done | bytes 786456
  2.9 56.6 %shard_map.28 = f32[80,768]{1,0:T(8,128)S(1)} custom-call(bf16[512,2560]{1,0:T(8,128)(2,1)S(1)} %copy-done, bf16[512,768]{1,0:T(8,128)(2,1)S(1)} %copy-done.1), custom_call_target="tpu_custom_call" | custom-call | tf_op jit(solution)/shard_map/pallas_call | solution.py:524
  59.5 0.7 %copy.4 = f32[80,768]{1,0:T(8,128)} copy(f32[80,768]{1,0:T(8,128)S(1)} %shard_map.28) | data formatting | bytes 491520
Async XLA Ops:
  0.0 1.7 %copy-start = (bf16[512,2560]{1,0:T(8,128)(2,1)S(1)}, bf16[512,2560]{1,0:T(8,128)(2,1)}, u32[]{:S(2)}) copy-start(bf16[512,2560]{1,0:T(8,128)(2,1)} %x_hbm.1) | copy-start | bytes 7864324
  1.7 1.1 %copy-start.1 = (bf16[512,768]{1,0:T(8,128)(2,1)S(1)}, bf16[512,768]{1,0:T(8,128)(2,1)}, u32[]{:S(2)}) copy-start(bf16[512,768]{1,0:T(8,128)(2,1)} %g_hbm.1) | copy-start | bytes 2359300
where the time goes:
time: 60.3 us; the launch traced here: 60.2 us
  Pallas kernels  56.6 us (94%)
  local copies, waits for them, and re-layouts  3.57 us (6%)
    pallas_call x1, Pallas kernels, per_device(): pl.pallas_call(functools.partial(kernel, groups, width, tokens * devices,...  56.6 us
    unnamed x5, local copies, waits for them, and re-layouts  3.57 us

commit v1 on v0

--- a/solution.py
+++ b/solution.py
@@ -15,7 +15,10 @@
 NG = R // BLK
 QROWS = D // 4
 QBLK = QROWS // BLK
-HALF = QROWS // 2
+CH = 4
+PART = BLK // CH
+SUB = PART // 2
+SROWS = QBLK * SUB
 CCOLS = R // 2
 CBLK = CCOLS // BLK
 SLOTS = 4
@@ -40,14 +43,21 @@
 def dot3(a, b):
     ah, al = split(a)
     bh, bl = split(b)
-    return dot(jnp.concatenate([ah, ah, al], axis=1), jnp.concatenate([bh, bl, bh], axis=0))
+    both = dot(
+        jnp.concatenate([ah, al], axis=1),
+        jnp.concatenate(
+            [jnp.concatenate([bh, bl], axis=1), jnp.concatenate([bh, jnp.zeros_like(bh)], axis=1)],
+            axis=0,
+        ),
+    )
+    return both[:, :BLK] + both[:, BLK:]
 
 
 def kernel(
     groups, width, total, rows,
     x_hbm, g_hbm, out_ref,
     x_ref, g_ref, xt, fpart, f1recv, f2send, f2recv, f3send, f3recv,
-    m1send, m1recv, macc, m2a, m2s, m2b, mq,
+    m1send, m1recv, mown, masend, m2a, mbsend, m2b,
     zsend, zrecv, inv_own, inv_a, inv_g, nat, fin_send, fin_recv, qsend, q1recv, q2recv,
     in_sem,
     f1_ss, f1_rs, f2_ss, f2_rs, f3_ss, f3_rs, m1_ss, m1_rs, ma_ss, ma_rs,
@@ -109,6 +119,98 @@
 
     zero = jnp.zeros((BLK, BLK), BF16)
     g_in.wait()
+    g_other = g_ref[:, pl.ds(pl.multiple_of((1 - core) * CCOLS, BLK), CCOLS)]
+    g_mine = g_ref[:, pl.ds(pl.multiple_of(core * CCOLS, BLK), CCOLS)]
+    for i in range(QBLK * CBLK, zslots * rest_n):
+        for k in range(CH):
+            zsend[k, i // zslots, i % zslots] = zero[:PART]
+
+    def scatter(ref, yq, xq, t, value):
+        for k in range(CH):
+            for h in range(2):
+                major, minor = (xq, yq) if h == 0 else (yq, xq)
+                start = k * PART + h * SUB
+                ref[k, h, major, minor, t * SUB:(t + 1) * SUB, :] = value[start:start + SUB]
+
+    for part in range(4):
+        x_in[part].wait()
+        for b in range(part * QBLK, (part + 1) * QBLK):
+            yq, xq, t = b // (2 * QBLK), b % 2, b % (2 * QBLK) // 2
+            xbt = x_ref[:, b * BLK:(b + 1) * BLK].T
+            xt[b] = xbt
+            scatter(m1send, yq, xq, t, dot(xbt, g_other).astype(BF16))
+
+    pl.semaphore_wait(barrier, rest_n + 3)
+    other = at(y, x, rest, 1 - core)
+    at_x = at(y, 1 - x, rest, core)
+    at_y = at(1 - y, x, rest, core)
+    m1 = [rcopy(m1send.at[k], m1recv.at[k], m1_ss.at[k], m1_rs.at[k], other) for k in range(CH)]
+    for cp in m1:
+        cp.start()
+
+    for b in range(NA):
+        yq, xq, t = b // (2 * QBLK), b % 2, b % (2 * QBLK) // 2
+        scatter(mown, yq, xq, t, dot(xt[b], g_mine))
+
+    def summed(k, h, major, minor):
+        return mown[k, h, major, minor] + m1recv[k, h, major, minor].astype(F32)
+
+    side = (x, y)
+    near = (at_x, at_y)
+    ma, mb = {}, {}
+
+    def stage_a(k):
+        m1[k].wait_recv()
+        for h in range(2):
+            for minor in range(2):
+                masend[k, h, minor] = summed(k, h, 1 - side[h], minor).astype(BF16)
+            ma[k, h] = rcopy(
+                masend.at[k, h], m2a.at[k, h], ma_ss.at[2 * k + h], ma_rs.at[2 * k + h], near[h]
+            )
+            ma[k, h].start()
+
+    def stage_b(k):
+        for h in range(2):
+            ma[k, h].wait_recv()
+            minor = 1 - side[1 - h]
+            mbsend[k, h] = (
+                summed(k, h, side[h], minor) + m2a[k, h, minor].astype(F32)
+            ).astype(BF16)
+            mb[k, h] = rcopy(
+                mbsend.at[k, h], m2b.at[k, h], mb_ss.at[2 * k + h], mb_rs.at[2 * k + h], near[1 - h]
+            )
+            mb[k, h].start()
+
+    def z_copy(k, dst, src):
+        return rcopy(
+            zsend.at[k, dst], zrecv.at[k, src],
+            z_ss.at[k * rest_n + dst], z_rs.at[k * rest_n + src], at(y, x, dst, core),
+        )
+
+    def stage_z(k):
+        for h in range(2):
+            mb[k, h].wait_recv()
+            minor = side[1 - h]
+            value = (
+                summed(k, h, side[h], minor) + m2a[k, h, minor].astype(F32) + m2b[k, h].astype(F32)
+            ) * (1.0 / total)
+            value = value.astype(BF16)
+            for i in range(QBLK * CBLK):
+                t, c = divmod(i, CBLK)
+                zsend[k, i // zslots, i % zslots, h * SUB:(h + 1) * SUB, :] = (
+                    value[t * SUB:(t + 1) * SUB, c * BLK:(c + 1) * BLK]
+                )
+
+        @pl.loop(0, rest_n)
+        def _(z):
+            @pl.when(z != rest)
+            def _():
+                z_copy(k, z, rest).start()
+
+        zrecv[k, rest] = zsend[k, rest]
+
+    stage_a(0)
+
     for c in range(NG):
         gb = g_ref[:, c * BLK:(c + 1) * BLK]
         fg = dot_t(gb, gb).astype(BF16)
@@ -120,33 +222,13 @@
         fpart[1, c, 3] = zero
         if c >= NG - 4:
             fpart[0, c, 3] = zero
-
-    for part in range(4):
-        x_in[part].wait()
-        for b in range(part * QBLK, (part + 1) * QBLK):
-            qq, t = b // (2 * QBLK) * 2 + b % 2, b % (2 * QBLK) // 2
-            xb = x_ref[:, b * BLK:(b + 1) * BLK]
-            xbt = xb.T
-            xt[qq * QBLK + t] = xbt
-            fpart[t % 2, qq, t // 2] = dot(xbt, xb).astype(BF16)
-
-    pl.semaphore_wait(barrier, rest_n + 3)
-    other = at(y, x, rest, 1 - core)
+    for b in range(NA):
+        qq, t = b // (2 * QBLK) * 2 + b % 2, b % (2 * QBLK) // 2
+        fpart[t % 2, qq, t // 2] = dot(xt[b], x_ref[:, b * BLK:(b + 1) * BLK]).astype(BF16)
     f1 = rcopy(fpart.at[1 - core], f1recv, f1_ss.at[0], f1_rs.at[0], other)
     f1.start()
 
-    g_other = g_ref[:, pl.ds(pl.multiple_of((1 - core) * CCOLS, BLK), CCOLS)]
-
-    def m1_copy(qq):
-        return rcopy(m1send.at[qq], m1recv.at[qq], m1_ss.at[qq], m1_rs.at[qq], other)
-
-    @pl.loop(1, 5)
-    def _(turn):
-        qq = lax.rem(q + turn, 4)
-        for t in range(QBLK):
-            m1send[qq, t * BLK:(t + 1) * BLK, :] = dot(xt[qq * QBLK + t], g_other).astype(BF16)
-        m1_copy(qq).start()
-
+    stage_a(1)
     f1.wait_recv()
 
     def f1_sum(qq, s):
@@ -162,38 +244,9 @@
         c2.start()
         f2.append(c2)
 
-    g_mine = g_ref[:, pl.ds(pl.multiple_of(core * CCOLS, BLK), CCOLS)]
-
-    at_x = at(y, 1 - x, rest, core)
-    at_y = at(1 - y, x, rest, core)
-
-    def ma_copy(i, h):
-        quarter = 2 * i + (1 - x) if h == 0 else 2 * (1 - y) + i
-        k = 2 * h + i
-        return rcopy(
-            macc.at[quarter, pl.ds(h * HALF, HALF)], m2a.at[k],
-            ma_ss.at[k], ma_rs.at[k], at_x if h == 0 else at_y,
-        )
-
-    @pl.loop(1, 5)
-    def _(turn):
-        qq = lax.rem(q + turn, 4)
-        m1_copy(qq).wait_recv()
-        for t in range(QBLK):
-            part = dot(xt[qq * QBLK + t], g_mine)
-            sl = slice(t * BLK, (t + 1) * BLK)
-            macc[qq, sl, :] = (part + m1recv[qq, sl, :].astype(F32)).astype(BF16)
-        yq, xq = lax.div(qq, 2), lax.rem(qq, 2)
-
-        @pl.when(xq != x)
-        def _():
-            ma_copy(yq, 0).start()
-
-        @pl.when(yq != y)
-        def _():
-            ma_copy(xq, 1).start()
-
-    ma = [ma_copy(i, h) for i in range(2) for h in range(2)]
+    stage_a(2)
+    stage_a(3)
+    stage_b(0)
 
     for c2 in f2:
         c2.wait_recv()
@@ -212,6 +265,9 @@
             f3_copy(s, rest).start()
 
     f3recv[rest] = f3send[lax.rem(rest, SLOTS)]
+
+    stage_b(1)
+    stage_z(0)
 
     @pl.when(rest < SLOTS)
     def _():
@@ -241,29 +297,24 @@
     damped = factor + (0.1 * (trace / BLK + 1e-06)) * eye
     peak = jnp.max(jnp.sum(jnp.abs(damped), axis=1, keepdims=True), axis=0, keepdims=True)
     scale = 1.0 / peak
-    approx = scale * (2.0 * eye - scale * damped)
-    for _ in range(ITERS - 5):
-        approx = dot3(approx, 2.0 * eye - dot3(damped, approx))
-
-    for ca in ma:
-        ca.wait_recv()
-    for i in range(2):
-        for h in range(2):
-            k = 2 * h + i
-            quarter = 2 * i + x if h == 0 else 2 * y + i
-            m2s[k] = (
-                macc[quarter, h * HALF:(h + 1) * HALF, :].astype(F32) + m2a[k].astype(F32)
-            ).astype(BF16)
-    mb = [
-        rcopy(m2s.at[1 - y], m2b.at[0], mb_ss.at[0], mb_rs.at[0], at_y),
-        rcopy(m2s.at[2 + 1 - x], m2b.at[1], mb_ss.at[1], mb_rs.at[1], at_x),
-    ]
-    for cb in mb:
-        cb.start()
-
-    for _ in range(4):
-        approx = dot3(approx, 2.0 * eye - dot3(damped, approx))
+    power = eye - scale * damped
+    approx = scale * (eye + power)
+    power = dot3(power, power)
+
+    def steps(n, power, approx):
+        for _ in range(n):
+            both = dot3(jnp.concatenate([power, approx], axis=0), power)
+            power, approx = both[:BLK], approx + both[BLK:]
+        return power, approx
+
+    power, approx = steps(2, power, approx)
+    stage_b(2)
+    stage_z(1)
+    power, approx = steps(4, power, approx)
+    approx = approx + dot3(approx, power)
     inv_own[...] = approx.astype(BF16)
+    stage_b(3)
+    stage_z(2)
 
     slot = 2 * rest + core
     is_a = slot < QBLK
@@ -309,51 +360,30 @@
         def _():
             inv_g[lax.rem(gidx, CBLK)] = inv_own[...]
 
-    for cb in mb:
-        cb.wait_recv()
-    for h in range(2):
-        kept = m2s[y] if h == 0 else m2s[2 + x]
-        mq[h * HALF:(h + 1) * HALF, :] = (
-            (kept.astype(F32) + m2b[h].astype(F32)) * (1.0 / total)
-        ).astype(BF16)
-
-    for i in range(zslots * rest_n):
-        t, c = divmod(i, CBLK)
-        tile = zero if t >= QBLK else mq[t * BLK:(t + 1) * BLK, c * BLK:(c + 1) * BLK]
-        zsend[i // zslots, i % zslots] = tile
-
-    def z_copy(dst, src):
-        return rcopy(zsend.at[dst], zrecv.at[src], z_ss.at[dst], z_rs.at[src], at(y, x, dst, core))
+    stage_z(3)
+
+    for c in range(CBLK):
+        @pl.when(jnp.logical_not(jnp.logical_and(is_g, gidx == core * CBLK + c)))
+        def _():
+            g_copy(0, c).wait_recv()
+    for t in range(QBLK):
+        @pl.when(slot != t)
+        def _():
+            a_copy(0, t).wait_recv()
 
     @pl.loop(0, rest_n)
     def _(z):
         @pl.when(z != rest)
         def _():
-            z_copy(z, rest).start()
-
-    zrecv[rest] = zsend[rest]
-
-    for c in range(CBLK):
-        @pl.when(jnp.logical_not(jnp.logical_and(is_g, gidx == core * CBLK + c)))
-        def _():
-            g_copy(0, c).wait_recv()
-    for t in range(QBLK):
-        @pl.when(slot != t)
-        def _():
-            a_copy(0, t).wait_recv()
-
-    @pl.loop(0, rest_n)
-    def _(z):
-        @pl.when(z != rest)
-        def _():
-            z_copy(0, z).wait_recv()
+            for k in range(CH):
+                z_copy(k, 0, z).wait_recv()
 
     square = jnp.zeros((1, 1), F32)
     for k in range(zslots):
         tile = rest * zslots + k
-        m = zrecv[0, k].astype(F32)
-        for z in range(1, rest_n):
-            m = m + zrecv[z, k].astype(F32)
+        m = jnp.concatenate(
+            [sum(zrecv[j, z, k].astype(F32) for z in range(rest_n)) for j in range(CH)], axis=0
+        )
         left = dot_t(inv_a[jnp.minimum(lax.div(tile, CBLK), QBLK - 1)], m.astype(BF16))
         hi, lo = split(left)
         ginv = inv_g[lax.rem(tile, CBLK)]
@@ -466,12 +496,8 @@
         out_ref[:, c * BLK:(c + 1) * BLK] = natural[:rows, :] * factor_out
 
     f1.wait_send()
-    for cp in f2 + ma + mb:
+    for cp in f2 + m1 + list(ma.values()) + list(mb.values()):
         cp.wait_send()
-
-    @pl.loop(0, 4)
-    def _(qq):
-        m1_copy(qq).wait_send()
 
     for s in range(SLOTS):
         @pl.when(rest != s)
@@ -494,7 +520,8 @@
             def _():
                 g_copy(i, 0).wait_send()
 
-    others(rest_n, rest, lambda z: z_copy(z, 0).wait_send())
+    for k in range(CH):
+        others(rest_n, rest, lambda z: z_copy(k, z, 0).wait_send())
     others(8, plane, lambda p: q1_copy(p, 0).wait_send())
     others(rest_n, rest, lambda z: q2_copy(z, 0).wait_send())
 
@@ -518,7 +545,8 @@
     pieces = max(
         ((t + 1) * BLK + rows - 1) // rows - t * BLK // rows for t in range(2 * QBLK)
     )
-    sems = [5, 1, 1, 3, 3, SLOTS, rest_n, 4, 4, 4, 4, 2, 2, rest_n, rest_n, max(owners, 4 * rest_n),
+    sems = [5, 1, 1, 3, 3, SLOTS, rest_n, CH, CH, 2 * CH, 2 * CH, 2 * CH, 2 * CH,
+            CH * rest_n, CH * rest_n, max(owners, 4 * rest_n),
             QBLK + CBLK, zslots * pieces, 2 * NG, 8, 8, rest_n, rest_n]
     vm = pltpu.VMEM
     return pl.pallas_call(
@@ -536,15 +564,15 @@
             vm((3, SLOTS) + blk, BF16),
             vm((SLOTS,) + blk, BF16),
             vm((rest_n,) + blk, BF16),
-            vm((4, QROWS, CCOLS), BF16),
-            vm((4, QROWS, CCOLS), BF16),
-            vm((4, QROWS, CCOLS), BF16),
-            vm((4, HALF, CCOLS), BF16),
-            vm((4, HALF, CCOLS), BF16),
-            vm((2, HALF, CCOLS), BF16),
-            vm((QROWS, CCOLS), BF16),
-            vm((rest_n, zslots) + blk, BF16),
-            vm((rest_n, zslots) + blk, BF16),
+            vm((CH, 2, 2, 2, SROWS, CCOLS), BF16),
+            vm((CH, 2, 2, 2, SROWS, CCOLS), BF16),
+            vm((CH, 2, 2, 2, SROWS, CCOLS), F32),
+            vm((CH, 2, 2, SROWS, CCOLS), BF16),
+            vm((CH, 2, 2, SROWS, CCOLS), BF16),
+            vm((CH, 2, SROWS, CCOLS), BF16),
+            vm((CH, 2, SROWS, CCOLS), BF16),
+            vm((CH, rest_n, zslots, PART, BLK), BF16),
+            vm((CH, rest_n, zslots, PART, BLK), BF16),
             vm(blk, BF16),
             vm((QBLK,) + blk, BF16),
             vm((CBLK,) + blk, BF16),
@@ -556,7 +584,7 @@
             vm((rest_n, 8, 128), F32),
         ] + [pltpu.SemaphoreType.DMA((n,)) for n in sems],
         compiler_params=pltpu.CompilerParams(
-            collective_id=0, has_side_effects=True, vmem_limit_bytes=48 * 1024 * 1024
+            collective_id=0, has_side_effects=True, vmem_limit_bytes=63 * 1024 * 1024
         ),
     )(acts, cotangents)
 

time: 60.3 us -> 59.3 us (0.983)
  local copies, waits for them, and re-layouts: 3.57 us -> 1.65 us
  Pallas kernels: 56.6 us -> 57.5 us
    unnamed x5 -> x1, local copies, waits for them, and re-layouts: 3.57 us -> 1.65 us
    pallas_call x1, Pallas kernels: 56.6 us -> 57.5 us  [per_device(): pl.pallas_call(functools.partial(kernel, groups, width, tokens * devices,...]
where the time goes in v1:
time: 59.3 us; the launch traced here: 59.2 us
  Pallas kernels  57.5 us (97%)
  local copies, waits for them, and re-layouts  1.65 us (3%)
    pallas_call x1, Pallas kernels, per_device(): pl.pallas_call(functools.partial(kernel, groups, width, tokens * devices,...  57.5 us
    unnamed x1, local copies, waits for them, and re-layouts  1.65 us

profile of v1, /device:TPU:0, one launch (start us, length us, event | category | flops | bytes accessed | tf_op | source)
XLA Modules:
  0.0 59.2 jit_solution(18216407058026717735)
XLA Ops:
  0.0 57.5 %shard_map.28 = f32[80,768]{1,0:T(8,128)} custom-call(bf16[512,2560]{1,0:T(8,128)(2,1)} %x_hbm.1, bf16[512,768]{1,0:T(8,128)(2,1)} %g_hbm.1), custom_call_target="tpu_custom_call" | custom-call | tf_op jit(solution)/shard_map/pallas_call | solution.py:552
  57.5 1.7 %copy.4 = f32[80,768]{1,0:T(8,128)} copy(f32[80,768]{1,0:T(8,128)} %shard_map.28) | data formatting | bytes 491520

commit v2 on v1

--- a/solution.py
+++ b/solution.py
@@ -21,7 +21,9 @@
 SROWS = QBLK * SUB
 CCOLS = R // 2
 CBLK = CCOLS // BLK
-SLOTS = 4
+PROWS = BLK + 16
+A_OWNER = ((0, 1, 0), (0, 1, 1), (1, 2, 0), (1, 2, 1), (0, 2, 0))
+G_OWNER = ((0, 2, 1), (1, 1, 0))
 MESH = pl.DeviceIdType.MESH
 F32 = jnp.float32
 BF16 = jnp.bfloat16
@@ -58,14 +60,13 @@
     x_hbm, g_hbm, out_ref,
     x_ref, g_ref, xt, fpart, f1recv, f2send, f2recv, f3send, f3recv,
     m1send, m1recv, mown, masend, m2a, mbsend, m2b,
-    zsend, zrecv, inv_own, inv_a, inv_g, nat, fin_send, fin_recv, qsend, q1recv, q2recv,
+    zsend, zrecv, state, inv_own, inv_a, inv_g, nat, fin_send, fin_recv, qsend, q1recv, q2recv,
     in_sem,
     f1_ss, f1_rs, f2_ss, f2_rs, f3_ss, f3_rs, m1_ss, m1_rs, ma_ss, ma_rs,
-    mb_ss, mb_rs, z_ss, z_rs, inv_ss, inv_rs, fin_ss, fin_rs, q1_ss, q1_rs, q2_ss, q2_rs,
+    mb_ss, mb_rs, z_ss, z_rs, inv_ss, inv_rs, gz_ss, gp_ss, g_rs, fin_ss, fin_rs, q1_ss, q1_rs, q2_ss, q2_rs,
 ):
     devices = groups * width
     rest_n = devices // 8
-    owners = devices // 4
     half_n = devices // 2
     zslots = zsend.shape[1]
     pieces = fin_send.shape[0] // zslots
@@ -132,18 +133,57 @@
                 start = k * PART + h * SUB
                 ref[k, h, major, minor, t * SUB:(t + 1) * SUB, :] = value[start:start + SUB]
 
+    if zslots * rest_n > QBLK * CBLK:
+        @pl.when(rest * zslots >= QBLK * CBLK)
+        def _():
+            inv_a[QBLK - 1] = zero
+
+    row = lax.broadcasted_iota(jnp.int32, (BLK, BLK), 0)
+    col = lax.broadcasted_iota(jnp.int32, (BLK, BLK), 1)
+    eye = (row == col).astype(F32)
+
+    def pack(ref, first, second):
+        ref[:BLK, :] = jnp.where(col >= row, first, second).astype(BF16)
+        diag = jnp.sum(second * eye, axis=0, keepdims=True)
+        ref[BLK:, :] = jnp.broadcast_to(diag, (PROWS - BLK, BLK)).astype(BF16)
+
+    def gram(c):
+        gb = g_ref[:, c * BLK:(c + 1) * BLK]
+        return dot_t(gb, gb)
+
+    for qq in range(NG - 4):
+        last = gram(4 + qq)
+        pack(fpart.at[1, qq, 0], last, last)
+    for qq in range(NG - 4, 4):
+        fpart[1, qq, 0] = jnp.zeros((PROWS, BLK), BF16)
+
+    held = {}
     for part in range(4):
         x_in[part].wait()
         for b in range(part * QBLK, (part + 1) * QBLK):
             yq, xq, t = b // (2 * QBLK), b % 2, b % (2 * QBLK) // 2
-            xbt = x_ref[:, b * BLK:(b + 1) * BLK].T
+            qq = 2 * yq + xq
+            xb = x_ref[:, b * BLK:(b + 1) * BLK]
+            xbt = xb.T
             xt[b] = xbt
-            scatter(m1send, yq, xq, t, dot(xbt, g_other).astype(BF16))
+            held[t] = held.get(t, {})
+            held[t][qq] = dot(xbt, xb)
+            if t == 1:
+                pack(fpart.at[0, qq, 0], held[0][qq], held[1][qq])
+            elif t == 3:
+                pack(fpart.at[1, qq, 1], held[2][qq], held[3][qq])
+            elif t == 4:
+                pack(fpart.at[0, qq, 1], held[4][qq], gram(qq))
+    for b in range(NA):
+        yq, xq, t = b // (2 * QBLK), b % 2, b % (2 * QBLK) // 2
+        scatter(m1send, yq, xq, t, dot(xt[b], g_other).astype(BF16))
 
     pl.semaphore_wait(barrier, rest_n + 3)
     other = at(y, x, rest, 1 - core)
     at_x = at(y, 1 - x, rest, core)
     at_y = at(1 - y, x, rest, core)
+    f1 = rcopy(fpart.at[1 - core], f1recv, f1_ss.at[0], f1_rs.at[0], other)
+    f1.start()
     m1 = [rcopy(m1send.at[k], m1recv.at[k], m1_ss.at[k], m1_rs.at[k], other) for k in range(CH)]
     for cp in m1:
         cp.start()
@@ -209,167 +249,206 @@
 
         zrecv[k, rest] = zsend[k, rest]
 
-    stage_a(0)
-
-    for c in range(NG):
-        gb = g_ref[:, c * BLK:(c + 1) * BLK]
-        fg = dot_t(gb, gb).astype(BF16)
-        if c < 4:
-            fpart[1, c, 2] = fg
-        else:
-            fpart[0, c - 4, 3] = fg
-    for c in range(4):
-        fpart[1, c, 3] = zero
-        if c >= NG - 4:
-            fpart[0, c, 3] = zero
-    for b in range(NA):
-        qq, t = b // (2 * QBLK) * 2 + b % 2, b % (2 * QBLK) // 2
-        fpart[t % 2, qq, t // 2] = dot(xt[b], x_ref[:, b * BLK:(b + 1) * BLK]).astype(BF16)
-    f1 = rcopy(fpart.at[1 - core], f1recv, f1_ss.at[0], f1_rs.at[0], other)
-    f1.start()
-
-    stage_a(1)
     f1.wait_recv()
 
     def f1_sum(qq, s):
         return fpart[core, qq, s].astype(F32) + f1recv[qq, s].astype(F32)
 
+    def present(yy, s):
+        return True if s == 1 else jnp.logical_or(core == 0, yy == 0)
+
     chips = [(y, 1 - x), (1 - y, x), (1 - y, 1 - x)]
-    f2 = []
+
+    def f2_copy(k, s):
+        yy, xx = chips[k]
+        i = 2 * k + s
+        return rcopy(f2send.at[k, s], f2recv.at[k, s], f2_ss.at[i], f2_rs.at[i], at(yy, xx, rest, core))
+
     for k, (yy, xx) in enumerate(chips):
-        qq = 2 * yy + xx
-        for s in range(SLOTS):
-            f2send[k, s] = f1_sum(qq, s).astype(BF16)
-        c2 = rcopy(f2send.at[k], f2recv.at[k], f2_ss.at[k], f2_rs.at[k], at(yy, xx, rest, core))
-        c2.start()
-        f2.append(c2)
-
+        for s in range(2):
+            @pl.when(present(yy, s))
+            def _():
+                f2send[k, s] = f1_sum(2 * yy + xx, s).astype(BF16)
+                f2_copy(k, s).start()
+
+    def f3_copy(s, src):
+        return rcopy(f3send.at[s], f3recv.at[src], f3_ss.at[s], f3_rs.at[src], at(y, x, s + 1, core))
+
+    def stage_f2():
+        for s in range(2):
+            @pl.when(present(y, s))
+            def _():
+                f = f1_sum(q, s)
+                for k in range(3):
+                    f2_copy(k, s).wait_recv()
+                    f = f + f2recv[k, s].astype(F32)
+                f3send[s] = f.astype(BF16)
+
+                @pl.when(rest != s + 1)
+                def _():
+                    f3_copy(s, rest).start()
+
+                @pl.when(rest == s + 1)
+                def _():
+                    f3recv[s + 1] = f3send[s]
+
+    is_owner = jnp.logical_or(
+        rest == 2, jnp.logical_and(rest == 1, jnp.logical_or(core == 0, y == 0))
+    )
+
+    def advance(n):
+        pairs = [(state[i, 0], state[i, 1]) for i in range(2)]
+        for _ in range(n):
+            done = []
+            for power, approx in pairs:
+                both = dot3(jnp.concatenate([power, approx], axis=0), power)
+                done.append((both[:BLK], approx + both[BLK:]))
+            pairs = done
+        return pairs
+
+    def stage_f3():
+        @pl.when(is_owner)
+        def _():
+            @pl.loop(0, rest_n)
+            def _(z):
+                @pl.when(z != rest)
+                def _():
+                    f3_copy(0, z).wait_recv()
+
+            packed = f3recv[0].astype(F32)
+            for z in range(1, rest_n):
+                packed = packed + f3recv[z].astype(F32)
+            packed = packed * (1.0 / total)
+            half = packed[:BLK]
+            flip = half.T
+            first = jnp.where(col >= row, half, flip)
+            second = jnp.where(col > row, flip, jnp.where(col < row, half, packed[BLK:BLK + 1]))
+            for i, factor in enumerate((first, second)):
+                trace = jnp.sum(jnp.sum(factor * eye, axis=1, keepdims=True), axis=0, keepdims=True)
+                damped = factor + (0.1 * (trace / BLK + 1e-06)) * eye
+                peak = jnp.max(jnp.sum(jnp.abs(damped), axis=1, keepdims=True), axis=0, keepdims=True)
+                scale = 1.0 / peak
+                power = eye - scale * damped
+                state[i, 1] = scale * (eye + power)
+                state[i, 0] = dot3(power, power)
+
+    def stage_newton(n, last):
+        @pl.when(is_owner)
+        def _():
+            for i, (power, approx) in enumerate(advance(n)):
+                if last:
+                    inv_own[i] = (approx + dot3(approx, power)).astype(BF16)
+                else:
+                    state[i, 0] = power
+                    state[i, 1] = approx
+
+    def owned(owner):
+        return jnp.logical_and(core == owner[0], rest == owner[1])
+
+    def needs(t):
+        return range(t * CBLK // zslots, (t * CBLK + CBLK - 1) // zslots + 1)
+
+    a_sends = []
+    for t in range(QBLK):
+        for z in needs(t):
+            for cc in range(2):
+                if (cc, z) != A_OWNER[t][:2]:
+                    a_sends.append((t, z, cc))
+
+    def a_copy(i):
+        t, z, cc = a_sends[i]
+        return rcopy(inv_own.at[A_OWNER[t][2]], inv_a.at[t], inv_ss.at[i], inv_rs.at[t], at(y, x, z, cc))
+
+    def g_half(e):
+        return lax.div(q + 4 * e, CBLK)
+
+    def gz_copy(e, z):
+        return rcopy(
+            inv_own.at[G_OWNER[e][2]], inv_g.at[lax.rem(q + 4 * e, CBLK)], gz_ss.at[e * rest_n + z],
+            g_rs.at[lax.rem(q + 4 * e, CBLK)], at(y, x, z, g_half(e)),
+        )
+
+    def each_gz(body):
+        for e in range(2):
+            @pl.when(owned(G_OWNER[e]) if e == 0 else jnp.logical_and(owned(G_OWNER[e]), q < NG - 4))
+            def _():
+                @pl.loop(0, rest_n)
+                def _(z):
+                    @pl.when(jnp.logical_or(z != rest, g_half(e) != core))
+                    def _():
+                        body(e, z)
+
+    def stage_inv():
+        for i, (t, z, cc) in enumerate(a_sends):
+            @pl.when(owned(A_OWNER[t]))
+            def _():
+                a_copy(i).start()
+        each_gz(lambda e, z: gz_copy(e, z).start())
+        for t in range(QBLK):
+            if A_OWNER[t][1] in needs(t):
+                @pl.when(owned(A_OWNER[t]))
+                def _():
+                    inv_a[t] = inv_own[A_OWNER[t][2]]
+
+    def g_home(j):
+        return lax.rem(core * CBLK + j, 4)
+
+    def g_owned(j):
+        late = core * CBLK + j >= 4
+        return jnp.logical_or(
+            jnp.logical_and(late, owned(G_OWNER[1])),
+            jnp.logical_and(jnp.logical_not(late), owned(G_OWNER[0])),
+        )
+
+    def gp_copy(j, k):
+        yy, xx = chips[k]
+        return rcopy(inv_g.at[j], inv_g.at[j], gp_ss.at[3 * j + k], g_rs.at[j], at(yy, xx, rest, core))
+
+    def stage_relay():
+        for j in range(CBLK):
+            @pl.when(q == g_home(j))
+            def _():
+                @pl.when(g_owned(j))
+                def _():
+                    inv_g[j] = inv_own[1 - core]
+
+                @pl.when(jnp.logical_not(g_owned(j)))
+                def _():
+                    gp_copy(j, 0).wait_recv()
+
+                for k in range(3):
+                    gp_copy(j, k).start()
+
+    stage_a(0)
+    stage_a(1)
+    stage_f2()
+    stage_b(0)
     stage_a(2)
-    stage_a(3)
-    stage_b(0)
-
-    for c2 in f2:
-        c2.wait_recv()
-    for s in range(SLOTS):
-        f = f1_sum(q, s)
-        for k in range(3):
-            f = f + f2recv[k, s].astype(F32)
-        f3send[s] = f.astype(BF16)
-
-    def f3_copy(s, src):
-        return rcopy(f3send.at[s], f3recv.at[src], f3_ss.at[s], f3_rs.at[src], at(y, x, s, core))
-
-    for s in range(SLOTS):
-        @pl.when(rest != s)
-        def _():
-            f3_copy(s, rest).start()
-
-    f3recv[rest] = f3send[lax.rem(rest, SLOTS)]
-
+    stage_f3()
     stage_b(1)
     stage_z(0)
-
-    @pl.when(rest < SLOTS)
-    def _():
-        @pl.loop(0, rest_n)
-        def _(z):
-            @pl.when(z != rest)
-            def _():
-                f3_copy(0, z).wait_recv()
-
-    if rest_n > SLOTS:
-        @pl.when(rest >= SLOTS)
-        def _():
-            @pl.loop(0, rest_n)
-            def _(z):
-                f3recv[z] = zero
-
-    factor = f3recv[0].astype(F32)
-    for z in range(1, rest_n):
-        factor = factor + f3recv[z].astype(F32)
-    factor = factor * (1.0 / total)
-
-    eye = (
-        lax.broadcasted_iota(jnp.int32, (BLK, BLK), 0)
-        == lax.broadcasted_iota(jnp.int32, (BLK, BLK), 1)
-    ).astype(F32)
-    trace = jnp.sum(jnp.sum(factor * eye, axis=1, keepdims=True), axis=0, keepdims=True)
-    damped = factor + (0.1 * (trace / BLK + 1e-06)) * eye
-    peak = jnp.max(jnp.sum(jnp.abs(damped), axis=1, keepdims=True), axis=0, keepdims=True)
-    scale = 1.0 / peak
-    power = eye - scale * damped
-    approx = scale * (eye + power)
-    power = dot3(power, power)
-
-    def steps(n, power, approx):
-        for _ in range(n):
-            both = dot3(jnp.concatenate([power, approx], axis=0), power)
-            power, approx = both[:BLK], approx + both[BLK:]
-        return power, approx
-
-    power, approx = steps(2, power, approx)
+    stage_newton(3, False)
+    stage_a(3)
     stage_b(2)
+    stage_newton(3, True)
+    stage_inv()
     stage_z(1)
-    power, approx = steps(4, power, approx)
-    approx = approx + dot3(approx, power)
-    inv_own[...] = approx.astype(BF16)
     stage_b(3)
     stage_z(2)
-
-    slot = 2 * rest + core
-    is_a = slot < QBLK
-    is_g = jnp.logical_or(slot == QBLK, jnp.logical_and(slot == QBLK + 1, q < NG - 4))
-    gidx = (slot - QBLK) * 4 + q
-    ghalf = lax.div(gidx, CBLK)
-
-    def a_copy(i, t):
-        return rcopy(
-            inv_own, inv_a.at[t], inv_ss.at[i], inv_rs.at[t],
-            at(y, x, lax.div(i, 2), lax.rem(i, 2)),
-        )
-
-    def g_dev(i):
-        chip = lax.div(i, rest_n)
-        return at(lax.div(chip, 2), lax.rem(chip, 2), lax.rem(i, rest_n), ghalf)
-
-    def g_copy(i, c):
-        return rcopy(inv_own, inv_g.at[c], inv_ss.at[i], inv_rs.at[QBLK + c], g_dev(i))
-
-    def not_me(i):
-        gg, dd = g_dev(i)
-        return gg * width + dd != me
-
-    @pl.when(is_a)
-    def _():
-        @pl.loop(0, owners)
-        def _(i):
-            @pl.when(i != slot)
-            def _():
-                a_copy(i, slot).start()
-        inv_a[slot] = inv_own[...]
-
-    @pl.when(is_g)
-    def _():
-        @pl.loop(0, 4 * rest_n)
-        def _(i):
-            @pl.when(not_me(i))
-            def _():
-                g_copy(i, lax.rem(gidx, CBLK)).start()
-
-        @pl.when(ghalf == core)
-        def _():
-            inv_g[lax.rem(gidx, CBLK)] = inv_own[...]
-
+    stage_relay()
     stage_z(3)
 
-    for c in range(CBLK):
-        @pl.when(jnp.logical_not(jnp.logical_and(is_g, gidx == core * CBLK + c)))
-        def _():
-            g_copy(0, c).wait_recv()
+    for j in range(CBLK):
+        @pl.when(q != g_home(j))
+        def _():
+            gp_copy(j, 0).wait_recv()
     for t in range(QBLK):
-        @pl.when(slot != t)
-        def _():
-            a_copy(0, t).wait_recv()
+        @pl.when(jnp.logical_and(
+            jnp.logical_and(rest >= needs(t)[0], rest <= needs(t)[-1]),
+            jnp.logical_not(owned(A_OWNER[t])),
+        ))
+        def _():
+            rcopy(inv_own.at[0], inv_a.at[t], inv_ss.at[0], inv_rs.at[t], other).wait_recv()
 
     @pl.loop(0, rest_n)
     def _(z):
@@ -496,29 +575,27 @@
         out_ref[:, c * BLK:(c + 1) * BLK] = natural[:rows, :] * factor_out
 
     f1.wait_send()
-    for cp in f2 + m1 + list(ma.values()) + list(mb.values()):
+    for cp in m1 + list(ma.values()) + list(mb.values()):
         cp.wait_send()
-
-    for s in range(SLOTS):
-        @pl.when(rest != s)
+    for k, (yy, xx) in enumerate(chips):
+        for s in range(2):
+            @pl.when(present(yy, s))
+            def _():
+                f2_copy(k, s).wait_send()
+    for s in range(2):
+        @pl.when(jnp.logical_and(present(y, s), rest != s + 1))
         def _():
             f3_copy(s, rest).wait_send()
-
-    @pl.when(is_a)
-    def _():
-        @pl.loop(0, owners)
-        def _(i):
-            @pl.when(i != slot)
-            def _():
-                a_copy(i, 0).wait_send()
-
-    @pl.when(is_g)
-    def _():
-        @pl.loop(0, 4 * rest_n)
-        def _(i):
-            @pl.when(not_me(i))
-            def _():
-                g_copy(i, 0).wait_send()
+    for i, (t, z, cc) in enumerate(a_sends):
+        @pl.when(owned(A_OWNER[t]))
+        def _():
+            a_copy(i).wait_send()
+    each_gz(lambda e, z: gz_copy(e, z).wait_send())
+    for j in range(CBLK):
+        @pl.when(q == g_home(j))
+        def _():
+            for k in range(3):
+                gp_copy(j, k).wait_send()
 
     for k in range(CH):
         others(rest_n, rest, lambda z: z_copy(k, z, 0).wait_send())
@@ -537,7 +614,6 @@
     tokens = acts.shape[0]
     devices = groups * width
     rest_n = devices // 8
-    owners = devices // 4
     rows = D // devices
     padded = (rows + 15) // 16 * 16
     blk = (BLK, BLK)
@@ -545,9 +621,9 @@
     pieces = max(
         ((t + 1) * BLK + rows - 1) // rows - t * BLK // rows for t in range(2 * QBLK)
     )
-    sems = [5, 1, 1, 3, 3, SLOTS, rest_n, CH, CH, 2 * CH, 2 * CH, 2 * CH, 2 * CH,
-            CH * rest_n, CH * rest_n, max(owners, 4 * rest_n),
-            QBLK + CBLK, zslots * pieces, 2 * NG, 8, 8, rest_n, rest_n]
+    sems = [5, 1, 1, 6, 6, 2, rest_n, CH, CH, 2 * CH, 2 * CH, 2 * CH, 2 * CH,
+            CH * rest_n, CH * rest_n, 2 * CBLK * QBLK, QBLK,
+            2 * rest_n, 3 * CBLK, CBLK, zslots * pieces, 2 * NG, 8, 8, rest_n, rest_n]
     vm = pltpu.VMEM
     return pl.pallas_call(
         functools.partial(kernel, groups, width, tokens * devices, rows),
@@ -558,12 +634,12 @@
             vm((tokens, D), BF16),
             vm((tokens, R), BF16),
             vm((NA, BLK, tokens), BF16),
-            vm((2, 4, SLOTS) + blk, BF16),
-            vm((4, SLOTS) + blk, BF16),
-            vm((3, SLOTS) + blk, BF16),
-            vm((3, SLOTS) + blk, BF16),
-            vm((SLOTS,) + blk, BF16),
-            vm((rest_n,) + blk, BF16),
+            vm((2, 4, 2, PROWS, BLK), BF16),
+            vm((4, 2, PROWS, BLK), BF16),
+            vm((3, 2, PROWS, BLK), BF16),
+            vm((3, 2, PROWS, BLK), BF16),
+            vm((2, PROWS, BLK), BF16),
+            vm((rest_n, PROWS, BLK), BF16),
             vm((CH, 2, 2, 2, SROWS, CCOLS), BF16),
             vm((CH, 2, 2, 2, SROWS, CCOLS), BF16),
             vm((CH, 2, 2, 2, SROWS, CCOLS), F32),
@@ -573,7 +649,8 @@
             vm((CH, 2, SROWS, CCOLS), BF16),
             vm((CH, rest_n, zslots, PART, BLK), BF16),
             vm((CH, rest_n, zslots, PART, BLK), BF16),
-            vm(blk, BF16),
+            vm((2, 2) + blk, F32),
+            vm((2,) + blk, BF16),
             vm((QBLK,) + blk, BF16),
             vm((CBLK,) + blk, BF16),
             vm((zslots,) + blk, F32),

time: 59.3 us -> 48.4 us (0.82)
  Pallas kernels: 57.5 us -> 46.5 us
    pallas_call x1, Pallas kernels: 57.5 us -> 46.5 us  [per_device(): pl.pallas_call(functools.partial(kernel, groups, width, tokens * devices,...]
where the time goes in v2:
time: 48.4 us; the launch traced here: 48.2 us
  Pallas kernels  46.5 us (96%)
  local copies, waits for them, and re-layouts  1.65 us (3%)
    pallas_call x1, Pallas kernels, per_device(): pl.pallas_call(functools.partial(kernel, groups, width, tokens * devices,...  46.5 us
    unnamed x1, local copies, waits for them, and re-layouts  1.65 us

profile of v2, /device:TPU:0, one launch (start us, length us, event | category | flops | bytes accessed | tf_op | source)
XLA Modules:
  0.0 48.2 jit_solution(4433422729066494523)
XLA Ops:
  0.0 46.5 %shard_map.28 = f32[80,768]{1,0:T(8,128)} custom-call(bf16[512,2560]{1,0:T(8,128)(2,1)} %x_hbm.1, bf16[512,768]{1,0:T(8,128)(2,1)} %g_hbm.1), custom_call_target="tpu_custom_call" | custom-call | tf_op jit(solution)/shard_map/pallas_call | solution.py:628
  46.6 1.7 %copy.4 = f32[80,768]{1,0:T(8,128)} copy(f32[80,768]{1,0:T(8,128)} %shard_map.28) | data formatting | bytes 491520

commit v3 on v2

--- a/solution.py
+++ b/solution.py
@@ -58,12 +58,12 @@
 def kernel(
     groups, width, total, rows,
     x_hbm, g_hbm, out_ref,
-    x_ref, g_ref, xt, fpart, f1recv, f2send, f2recv, f3send, f3recv,
+    x_ref, g_ref, xt, fpart, f1recv, fzsend, fzrecv, f2send, f2recv,
     m1send, m1recv, mown, masend, m2a, mbsend, m2b,
-    zsend, zrecv, state, inv_own, inv_a, inv_g, nat, fin_send, fin_recv, qsend, q1recv, q2recv,
+    zsend, zrecv, state, inv_own, inv_a, inv_g, nat, fin_send, fin_recv, qsend, qrecv,
     in_sem,
-    f1_ss, f1_rs, f2_ss, f2_rs, f3_ss, f3_rs, m1_ss, m1_rs, ma_ss, ma_rs,
-    mb_ss, mb_rs, z_ss, z_rs, inv_ss, inv_rs, gz_ss, gp_ss, g_rs, fin_ss, fin_rs, q1_ss, q1_rs, q2_ss, q2_rs,
+    f1_ss, f1_rs, fz_ss, fz_rs, f2_ss, f2_rs, m1_ss, m1_rs, ma_ss, ma_rs,
+    mb_ss, mb_rs, z_ss, z_rs, inv_ss, inv_rs, gz_ss, gp_ss, g_rs, fin_ss, fin_rs, q_ss, q_rs,
 ):
     devices = groups * width
     rest_n = devices // 8
@@ -183,14 +183,12 @@
     at_x = at(y, 1 - x, rest, core)
     at_y = at(1 - y, x, rest, core)
     f1 = rcopy(fpart.at[1 - core], f1recv, f1_ss.at[0], f1_rs.at[0], other)
-    f1.start()
     m1 = [rcopy(m1send.at[k], m1recv.at[k], m1_ss.at[k], m1_rs.at[k], other) for k in range(CH)]
-    for cp in m1:
-        cp.start()
-
-    for b in range(NA):
-        yq, xq, t = b // (2 * QBLK), b % 2, b % (2 * QBLK) // 2
-        scatter(mown, yq, xq, t, dot(xt[b], g_mine))
+
+    def stage_own(part):
+        for b in range(part * QBLK, (part + 1) * QBLK):
+            yq, xq, t = b // (2 * QBLK), b % 2, b % (2 * QBLK) // 2
+            scatter(mown, yq, xq, t, dot(xt[b], g_mine))
 
     def summed(k, h, major, minor):
         return mown[k, h, major, minor] + m1recv[k, h, major, minor].astype(F32)
@@ -249,13 +247,8 @@
 
         zrecv[k, rest] = zsend[k, rest]
 
-    f1.wait_recv()
-
     def f1_sum(qq, s):
         return fpart[core, qq, s].astype(F32) + f1recv[qq, s].astype(F32)
-
-    def present(yy, s):
-        return True if s == 1 else jnp.logical_or(core == 0, yy == 0)
 
     chips = [(y, 1 - x), (1 - y, x), (1 - y, 1 - x)]
 
@@ -264,33 +257,70 @@
         i = 2 * k + s
         return rcopy(f2send.at[k, s], f2recv.at[k, s], f2_ss.at[i], f2_rs.at[i], at(yy, xx, rest, core))
 
-    for k, (yy, xx) in enumerate(chips):
+    def fz_copy(s, src, n):
+        return rcopy(
+            fzsend.at[s, pl.ds(0, n)], fzrecv.at[src, pl.ds(0, n)], fz_ss.at[s], fz_rs.at[src],
+            at(y, x, s + 1, core),
+        )
+
+    def with_count(here, s, body):
+        late = core if s is None else core * (1 - s)
+        if s is None:
+            late = core * (2 - rest)
+
+        @pl.when(jnp.logical_and(here, late == 1))
+        def _():
+            body(NG - 4)
+
+        @pl.when(jnp.logical_and(here, late != 1))
+        def _():
+            body(4)
+
+    def stage_f1():
+        f1.wait_recv()
         for s in range(2):
-            @pl.when(present(yy, s))
-            def _():
-                f2send[k, s] = f1_sum(2 * yy + xx, s).astype(BF16)
-                f2_copy(k, s).start()
-
-    def f3_copy(s, src):
-        return rcopy(f3send.at[s], f3recv.at[src], f3_ss.at[s], f3_rs.at[src], at(y, x, s + 1, core))
+            for qq in range(4):
+                fzsend[s, qq] = f1_sum(qq, s).astype(BF16)
+            with_count(rest != s + 1, s, lambda n: fz_copy(s, rest, n).start())
+
+            @pl.when(rest == s + 1)
+            def _():
+                fzrecv[s + 1] = fzsend[s]
+
+    hub = jnp.logical_or(rest == 1, rest == 2)
+
+    def column_sum(qq):
+        f = fzrecv[0, qq].astype(F32)
+        for z in range(1, rest_n):
+            f = f + fzrecv[z, qq].astype(F32)
+        return f
+
+    def f2_copy(k):
+        yy, xx = chips[k]
+        return rcopy(f2send.at[k], f2recv.at[k], f2_ss.at[k], f2_rs.at[k], at(yy, xx, rest, core))
+
+    def each_f2(body):
+        for k, (yy, xx) in enumerate(chips):
+            @pl.when(jnp.logical_or(
+                rest == 2, jnp.logical_and(rest == 1, jnp.logical_or(core == 0, yy == 0))
+            ))
+            def _():
+                body(k, 2 * yy + xx)
+
+    def send_f2(k, qq):
+        f2send[k] = column_sum(qq).astype(BF16)
+        f2_copy(k).start()
 
     def stage_f2():
-        for s in range(2):
-            @pl.when(present(y, s))
-            def _():
-                f = f1_sum(q, s)
-                for k in range(3):
-                    f2_copy(k, s).wait_recv()
-                    f = f + f2recv[k, s].astype(F32)
-                f3send[s] = f.astype(BF16)
-
-                @pl.when(rest != s + 1)
+        def wait(n):
+            @pl.loop(0, rest_n)
+            def _(z):
+                @pl.when(z != rest)
                 def _():
-                    f3_copy(s, rest).start()
-
-                @pl.when(rest == s + 1)
-                def _():
-                    f3recv[s + 1] = f3send[s]
+                    fz_copy(0, z, n).wait_recv()
+
+        with_count(hub, None, wait)
+        each_f2(send_f2)
 
     is_owner = jnp.logical_or(
         rest == 2, jnp.logical_and(rest == 1, jnp.logical_or(core == 0, y == 0))
@@ -309,15 +339,10 @@
     def stage_f3():
         @pl.when(is_owner)
         def _():
-            @pl.loop(0, rest_n)
-            def _(z):
-                @pl.when(z != rest)
-                def _():
-                    f3_copy(0, z).wait_recv()
-
-            packed = f3recv[0].astype(F32)
-            for z in range(1, rest_n):
-                packed = packed + f3recv[z].astype(F32)
+            packed = column_sum(q)
+            for k in range(3):
+                f2_copy(k).wait_recv()
+                packed = packed + f2recv[k].astype(F32)
             packed = packed * (1.0 / total)
             half = packed[:BLK]
             flip = half.T
@@ -419,16 +444,26 @@
                 for k in range(3):
                     gp_copy(j, k).start()
 
+    f1.start()
+    m1[0].start()
+    stage_own(0)
+    stage_own(1)
+    m1[1].start()
+    stage_own(2)
+    stage_own(3)
+    stage_f1()
     stage_a(0)
+    m1[2].start()
     stage_a(1)
-    stage_f2()
+    m1[3].start()
     stage_b(0)
     stage_a(2)
-    stage_f3()
+    stage_f2()
     stage_b(1)
     stage_z(0)
+    stage_a(3)
+    stage_f3()
     stage_newton(3, False)
-    stage_a(3)
     stage_b(2)
     stage_newton(3, True)
     stage_inv()
@@ -471,18 +506,13 @@
         square = square + jnp.sum(
             jnp.sum(part * part, axis=0, keepdims=True), axis=1, keepdims=True
         )
-    qsend[0] = jnp.broadcast_to(square, (8, 128))
-
-    def q1_copy(p, src):
-        return rcopy(
-            qsend.at[0], q1recv.at[src], q1_ss.at[p], q1_rs.at[src],
-            at(lax.div(p, 4), lax.rem(lax.div(p, 2), 2), rest, lax.rem(p, 2)),
-        )
-
-    def q2_copy(z, src):
-        return rcopy(qsend.at[1], q2recv.at[src], q2_ss.at[z], q2_rs.at[src], at(y, x, z, core))
-
-    plane = 2 * q + core
+    qsend[...] = jnp.broadcast_to(square, (1, 128))
+
+    def q_copy(p):
+        return rcopy(qsend, qrecv.at[me], q_ss.at[0], q_rs.at[0], linear(p))
+
+    rest_of = qrecv.at[pl.ds(0, devices - 1)]
+    q_all = rcopy(rest_of, rest_of, q_ss.at[0], q_rs.at[0], other)
 
     def others(n, mine, body):
         @pl.loop(0, n)
@@ -491,8 +521,8 @@
             def _():
                 body(p)
 
-    others(8, plane, lambda p: q1_copy(p, plane).start())
-    q1recv[plane] = qsend[0]
+    others(devices, me, lambda p: q_copy(p).start())
+    qrecv[me] = qsend[...]
 
     def each_piece(body):
         for xx in range(2):
@@ -533,11 +563,6 @@
             fin_recv[core * CBLK + c, late] = fin_send[j]
 
     each_piece(send_piece)
-
-    others(8, plane, lambda p: q1_copy(0, p).wait_recv())
-    qsend[1] = jnp.sum(q1recv[...], axis=0)
-    others(rest_n, rest, lambda z: q2_copy(z, rest).start())
-    q2recv[rest] = qsend[1]
 
     k_me = lax.rem(me, half_n)
     t_me = lax.div(k_me * rows, BLK)
@@ -567,8 +592,8 @@
                     recv_sem=fin_rs.at[2 * c + late], device_id=other, device_id_type=MESH,
                 ).wait_recv()
 
-    others(rest_n, rest, lambda z: q2_copy(0, z).wait_recv())
-    quad = jnp.sum(q2recv[...], axis=0)[:1, :1] / (D * R)
+    q_all.wait_recv()
+    quad = jnp.sum(qrecv[...], axis=0)[:1, :1] / (D * R)
     factor_out = lax.rsqrt(quad + 1e-06)
     for c in range(NG):
         natural = fin_recv[c, 0].astype(F32) + fin_recv[c, 1].astype(F32)
@@ -577,15 +602,9 @@
     f1.wait_send()
     for cp in m1 + list(ma.values()) + list(mb.values()):
         cp.wait_send()
-    for k, (yy, xx) in enumerate(chips):
-        for s in range(2):
-            @pl.when(present(yy, s))
-            def _():
-                f2_copy(k, s).wait_send()
     for s in range(2):
-        @pl.when(jnp.logical_and(present(y, s), rest != s + 1))
-        def _():
-            f3_copy(s, rest).wait_send()
+        with_count(rest != s + 1, s, lambda n: fz_copy(s, rest, n).wait_send())
+    each_f2(lambda k, qq: f2_copy(k).wait_send())
     for i, (t, z, cc) in enumerate(a_sends):
         @pl.when(owned(A_OWNER[t]))
         def _():
@@ -599,8 +618,7 @@
 
     for k in range(CH):
         others(rest_n, rest, lambda z: z_copy(k, z, 0).wait_send())
-    others(8, plane, lambda p: q1_copy(p, 0).wait_send())
-    others(rest_n, rest, lambda z: q2_copy(z, 0).wait_send())
+    q_all.wait_send()
 
     def wait_piece(slot_k, c, k, above, start, count, late, j):
         @pl.when(y * half_n + k != me)
@@ -621,9 +639,9 @@
     pieces = max(
         ((t + 1) * BLK + rows - 1) // rows - t * BLK // rows for t in range(2 * QBLK)
     )
-    sems = [5, 1, 1, 6, 6, 2, rest_n, CH, CH, 2 * CH, 2 * CH, 2 * CH, 2 * CH,
+    sems = [5, 1, 1, 2, rest_n, 3, 3, CH, CH, 2 * CH, 2 * CH, 2 * CH, 2 * CH,
             CH * rest_n, CH * rest_n, 2 * CBLK * QBLK, QBLK,
-            2 * rest_n, 3 * CBLK, CBLK, zslots * pieces, 2 * NG, 8, 8, rest_n, rest_n]
+            2 * rest_n, 3 * CBLK, CBLK, zslots * pieces, 2 * NG, 1, 1]
     vm = pltpu.VMEM
     return pl.pallas_call(
         functools.partial(kernel, groups, width, tokens * devices, rows),
@@ -636,10 +654,10 @@
             vm((NA, BLK, tokens), BF16),
             vm((2, 4, 2, PROWS, BLK), BF16),
             vm((4, 2, PROWS, BLK), BF16),
-            vm((3, 2, PROWS, BLK), BF16),
-            vm((3, 2, PROWS, BLK), BF16),
-            vm((2, PROWS, BLK), BF16),
-            vm((rest_n, PROWS, BLK), BF16),
+            vm((2, 4, PROWS, BLK), BF16),
+            vm((rest_n, 4, PROWS, BLK), BF16),
+            vm((3, PROWS, BLK), BF16),
+            vm((3, PROWS, BLK), BF16),
             vm((CH, 2, 2, 2, SROWS, CCOLS), BF16),
             vm((CH, 2, 2, 2, SROWS, CCOLS), BF16),
             vm((CH, 2, 2, 2, SROWS, CCOLS), F32),
@@ -656,9 +674,8 @@
             vm((zslots,) + blk, F32),
             vm((zslots * pieces, padded, BLK), BF16),
             vm((NG, 2, padded, BLK), BF16),
-            vm((2, 8, 128), F32),
-            vm((8, 8, 128), F32),
-            vm((rest_n, 8, 128), F32),
+            vm((1, 128), F32),
+            vm((devices, 1, 128), F32),
         ] + [pltpu.SemaphoreType.DMA((n,)) for n in sems],
         compiler_params=pltpu.CompilerParams(
             collective_id=0, has_side_effects=True, vmem_limit_bytes=63 * 1024 * 1024

time: 48.4 us -> 44.2 us (0.913)
  Pallas kernels: 46.5 us -> 42.4 us
    pallas_call x1, Pallas kernels: 46.5 us -> 42.4 us  [per_device(): pl.pallas_call(functools.partial(kernel, groups, width, tokens * devices,...]
where the time goes in v3:
time: 44.2 us; the launch traced here: 44.1 us
  Pallas kernels  42.4 us (96%)
  local copies, waits for them, and re-layouts  1.65 us (4%)
    pallas_call x1, Pallas kernels, per_device(): pl.pallas_call(functools.partial(kernel, groups, width, tokens * devices,...  42.4 us
    unnamed x1, local copies, waits for them, and re-layouts  1.65 us

profile of v3, /device:TPU:0, one launch (start us, length us, event | category | flops | bytes accessed | tf_op | source)
XLA Modules:
  0.0 44.1 jit_solution(3123381594217067417)
XLA Ops:
  0.0 42.4 %shard_map.28 = f32[80,768]{1,0:T(8,128)} custom-call(bf16[512,2560]{1,0:T(8,128)(2,1)} %x_hbm.1, bf16[512,768]{1,0:T(8,128)(2,1)} %g_hbm.1), custom_call_target="tpu_custom_call" | custom-call | tf_op jit(solution)/shard_map/pallas_call | solution.py:646
  42.5 1.7 %copy.4 = f32[80,768]{1,0:T(8,128)} copy(f32[80,768]{1,0:T(8,128)} %shard_map.28) | data formatting | bytes 491520

commit v4 on v3

--- a/solution.py
+++ b/solution.py
@@ -61,7 +61,7 @@
     x_ref, g_ref, xt, fpart, f1recv, fzsend, fzrecv, f2send, f2recv,
     m1send, m1recv, mown, masend, m2a, mbsend, m2b,
     zsend, zrecv, state, inv_own, inv_a, inv_g, nat, fin_send, fin_recv, qsend, qrecv,
-    in_sem,
+    know, in_sem,
     f1_ss, f1_rs, fz_ss, fz_rs, f2_ss, f2_rs, m1_ss, m1_rs, ma_ss, ma_rs,
     mb_ss, mb_rs, z_ss, z_rs, inv_ss, inv_rs, gz_ss, gp_ss, g_rs, fin_ss, fin_rs, q_ss, q_rs,
 ):
@@ -109,14 +109,35 @@
         pl.semaphore_signal(barrier, inc=1, device_id=dev, device_id_type=MESH)
 
     greet(at(y, x, rest, 1 - core))
-    for yy, xx in ((y, 1 - x), (1 - y, x), (1 - y, 1 - x)):
-        greet(at(yy, xx, rest, core))
-
-    @pl.loop(0, rest_n)
-    def _(z):
-        @pl.when(z != rest)
-        def _():
-            greet(at(y, x, z, core))
+    greet(at(y, 1 - x, rest, core))
+    greet(at(1 - y, x, rest, core))
+
+    def near_z(reach, body):
+        @pl.when(rest >= reach)
+        def _():
+            body(rest - reach)
+
+        @pl.when(rest + reach < rest_n)
+        def _():
+            body(rest + reach)
+
+    def sides(reach):
+        return (rest >= reach).astype(jnp.int32) + (rest + reach < rest_n).astype(jnp.int32)
+
+    near_z(1, lambda z: greet(at(y, x, z, core)))
+    rounds = (rest_n - 2).bit_length()
+    hub_rounds = (max(rest_n - 3, 1)).bit_length()
+
+    def tell(r):
+        near_z(1 << r, lambda z: pl.semaphore_signal(
+            know.at[r], inc=1, device_id=at(y, x, z, core), device_id_type=MESH
+        ))
+
+    def hear(first, last):
+        for r in range(first, last):
+            pl.semaphore_wait(know.at[r], sides(1 << r))
+            if r + 1 < rounds:
+                tell(r + 1)
 
     zero = jnp.zeros((BLK, BLK), BF16)
     g_in.wait()
@@ -178,7 +199,8 @@
         yq, xq, t = b // (2 * QBLK), b % 2, b % (2 * QBLK) // 2
         scatter(m1send, yq, xq, t, dot(xt[b], g_other).astype(BF16))
 
-    pl.semaphore_wait(barrier, rest_n + 3)
+    pl.semaphore_wait(barrier, 3 + sides(1))
+    tell(0)
     other = at(y, x, rest, 1 - core)
     at_x = at(y, 1 - x, rest, core)
     at_y = at(1 - y, x, rest, core)
@@ -225,7 +247,11 @@
             z_ss.at[k * rest_n + dst], z_rs.at[k * rest_n + src], at(y, x, dst, core),
         )
 
+    chips = [(y, 1 - x), (1 - y, x), (1 - y, 1 - x)]
+
     def stage_z(k):
+        if k == 0:
+            hear(hub_rounds, rounds)
         for h in range(2):
             mb[k, h].wait_recv()
             minor = side[1 - h]
@@ -250,7 +276,6 @@
     def f1_sum(qq, s):
         return fpart[core, qq, s].astype(F32) + f1recv[qq, s].astype(F32)
 
-    chips = [(y, 1 - x), (1 - y, x), (1 - y, 1 - x)]
 
     def f2_copy(k, s):
         yy, xx = chips[k]
@@ -277,6 +302,7 @@
             body(4)
 
     def stage_f1():
+        hear(0, hub_rounds)
         f1.wait_recv()
         for s in range(2):
             for qq in range(4):
@@ -444,15 +470,15 @@
                 for k in range(3):
                     gp_copy(j, k).start()
 
+    m1[0].start()
     f1.start()
-    m1[0].start()
     stage_own(0)
     stage_own(1)
     m1[1].start()
     stage_own(2)
     stage_own(3)
+    stage_a(0)
     stage_f1()
-    stage_a(0)
     m1[2].start()
     stage_a(1)
     m1[3].start()
@@ -460,13 +486,13 @@
     stage_a(2)
     stage_f2()
     stage_b(1)
+    stage_a(3)
     stage_z(0)
-    stage_a(3)
     stage_f3()
     stage_newton(3, False)
-    stage_b(2)
     stage_newton(3, True)
     stage_inv()
+    stage_b(2)
     stage_z(1)
     stage_b(3)
     stage_z(2)
@@ -676,6 +702,7 @@
             vm((NG, 2, padded, BLK), BF16),
             vm((1, 128), F32),
             vm((devices, 1, 128), F32),
+            pltpu.SemaphoreType.REGULAR((8,)),
         ] + [pltpu.SemaphoreType.DMA((n,)) for n in sems],
         compiler_params=pltpu.CompilerParams(
             collective_id=0, has_side_effects=True, vmem_limit_bytes=63 * 1024 * 1024

time: 44.2 us -> 43.9 us (level)
  no operation moved by 1% of the time
where the time goes in v4:
time: 43.9 us; the launch traced here: 43.8 us
  Pallas kernels  42.1 us (96%)
  local copies, waits for them, and re-layouts  1.65 us (4%)
    pallas_call x1, Pallas kernels, per_device(): pl.pallas_call(functools.partial(kernel, groups, width, tokens * devices,...  42.1 us
    unnamed x1, local copies, waits for them, and re-layouts  1.65 us

profile of v4, /device:TPU:0, one launch (start us, length us, event | category | flops | bytes accessed | tf_op | source)
XLA Modules:
  0.0 43.8 jit_solution(10087443610389302626)
XLA Ops:
  0.0 42.1 %shard_map.28 = f32[80,768]{1,0:T(8,128)} custom-call(bf16[512,2560]{1,0:T(8,128)(2,1)} %x_hbm.1, bf16[512,768]{1,0:T(8,128)(2,1)} %g_hbm.1), custom_call_target="tpu_custom_call" | custom-call | tf_op jit(solution)/shard_map/pallas_call | solution.py:672
  42.2 1.7 %copy.4 = f32[80,768]{1,0:T(8,128)} copy(f32[80,768]{1,0:T(8,128)} %shard_map.28) | data formatting | bytes 491520

commit v5 on v4

--- a/solution.py
+++ b/solution.py
@@ -472,14 +472,14 @@
 
     m1[0].start()
     f1.start()
+    m1[1].start()
     stage_own(0)
     stage_own(1)
-    m1[1].start()
     stage_own(2)
     stage_own(3)
+    m1[2].start()
     stage_a(0)
     stage_f1()
-    m1[2].start()
     stage_a(1)
     m1[3].start()
     stage_b(0)
@@ -491,8 +491,8 @@
     stage_f3()
     stage_newton(3, False)
     stage_newton(3, True)
+    stage_b(2)
     stage_inv()
-    stage_b(2)
     stage_z(1)
     stage_b(3)
     stage_z(2)

time: 43.9 us -> 43.9 us (level)
  no operation moved by 1% of the time
where the time goes in v5:
time: 43.9 us; the launch traced here: 43.7 us
  Pallas kernels  42.1 us (96%)
  local copies, waits for them, and re-layouts  1.65 us (4%)
    pallas_call x1, Pallas kernels, per_device(): pl.pallas_call(functools.partial(kernel, groups, width, tokens * devices,...  42.1 us
    unnamed x1, local copies, waits for them, and re-layouts  1.65 us

profile of v5, /device:TPU:0, one launch (start us, length us, event | category | flops | bytes accessed | tf_op | source)
XLA Modules:
  0.0 43.7 jit_solution(12658712579341546084)
XLA Ops:
  0.0 42.1 %shard_map.28 = f32[80,768]{1,0:T(8,128)} custom-call(bf16[512,2560]{1,0:T(8,128)(2,1)} %x_hbm.1, bf16[512,768]{1,0:T(8,128)(2,1)} %g_hbm.1), custom_call_target="tpu_custom_call" | custom-call | tf_op jit(solution)/shard_map/pallas_call | solution.py:672
  42.1 1.7 %copy.4 = f32[80,768]{1,0:T(8,128)} copy(f32[80,768]{1,0:T(8,128)} %shard_map.28) | data formatting | bytes 491520

commit v6 on v5

--- a/solution.py
+++ b/solution.py
@@ -518,7 +518,7 @@
             for k in range(CH):
                 z_copy(k, 0, z).wait_recv()
 
-    square = jnp.zeros((1, 1), F32)
+    square = jnp.zeros((BLK, BLK), F32)
     for k in range(zslots):
         tile = rest * zslots + k
         m = jnp.concatenate(
@@ -529,10 +529,8 @@
         ginv = inv_g[lax.rem(tile, CBLK)]
         part = dot(hi, ginv) + dot(lo, ginv)
         nat[k] = part
-        square = square + jnp.sum(
-            jnp.sum(part * part, axis=0, keepdims=True), axis=1, keepdims=True
-        )
-    qsend[...] = jnp.broadcast_to(square, (1, 128))
+        square = square + part * part
+    qsend[...] = jnp.sum(square, axis=0, keepdims=True)
 
     def q_copy(p):
         return rcopy(qsend, qrecv.at[me], q_ss.at[0], q_rs.at[0], linear(p))
@@ -619,7 +617,7 @@
                 ).wait_recv()
 
     q_all.wait_recv()
-    quad = jnp.sum(qrecv[...], axis=0)[:1, :1] / (D * R)
+    quad = jnp.sum(jnp.sum(qrecv[...], axis=0), axis=1, keepdims=True) / (D * R)
     factor_out = lax.rsqrt(quad + 1e-06)
     for c in range(NG):
         natural = fin_recv[c, 0].astype(F32) + fin_recv[c, 1].astype(F32)

time: 43.9 us -> 43.8 us (level)
  no operation moved by 1% of the time
where the time goes in v6:
time: 43.8 us; the launch traced here: 43.7 us
  Pallas kernels  42 us (96%)
  local copies, waits for them, and re-layouts  1.65 us (4%)
    pallas_call x1, Pallas kernels, per_device(): pl.pallas_call(functools.partial(kernel, groups, width, tokens * devices,...  42 us
    unnamed x1, local copies, waits for them, and re-layouts  1.65 us

profile of v6, /device:TPU:0, one launch (start us, length us, event | category | flops | bytes accessed | tf_op | source)
XLA Modules:
  0.0 43.7 jit_solution(11069662265329224457)
XLA Ops:
  0.0 42.0 %shard_map.28 = f32[80,768]{1,0:T(8,128)} custom-call(bf16[512,2560]{1,0:T(8,128)(2,1)} %x_hbm.1, bf16[512,768]{1,0:T(8,128)(2,1)} %g_hbm.1), custom_call_target="tpu_custom_call" | custom-call | tf_op jit(solution)/shard_map/pallas_call | solution.py:670
  42.0 1.7 %copy.4 = f32[80,768]{1,0:T(8,128)} copy(f32[80,768]{1,0:T(8,128)} %shard_map.28) | data formatting | bytes 491520
